TPU v7x, 32 devices: a whole 2x2x4 slice. The times are simulated.
32 devices in a mesh: expert: 16 (over z, y, core), narrow: 2 (over x).
Axes of the slice: x: 2, y: 2, z: 4, core: 2. Of those that a mesh axis runs over, the one named last changes fastest.
Arguments:
- tokens: bfloat16 [768, 4096], P('expert', 'narrow'), may hold values from -6 to 6
- route_ids: int32 [768, 8], P('expert'), may hold values from 0 to 15, all different within a row; in each aligned block of 48 rows (0 to 47, 48 to 95, ...) at most 48 rows name the same one
- route_weight: bfloat16 [768, 8], P('expert'), may hold values from 0.049804688 to 0.5
- partner: int32 [16], replicated, may hold values from 0 to 15, as said below
- old_place: int32 [16], replicated, may hold values from 0 to 15, each once
- gate_weight: bfloat16 [16, 768, 4096], P('expert', 'narrow'), may hold values from -0.09375 to 0.09375
- up_weight: bfloat16 [16, 768, 4096], P('expert', 'narrow'), may hold values from -0.09375 to 0.09375
- down_weight: bfloat16 [16, 768, 4096], P('expert', None, 'narrow'), may hold values from -0.21875 to 0.21875
Outputs:
- layer_out: bfloat16 [768, 4096], P('expert', 'narrow')
- new_gate: bfloat16 [16, 768, 4096], P('expert', 'narrow')
- new_up: bfloat16 [16, 768, 4096], P('expert', 'narrow')
- new_down: bfloat16 [16, 768, 4096], P('expert', None, 'narrow')
Inputs may be any that keep to these rules, and one draw needn't show every extreme that they name: partner[partner[s]] == s for every slot; slots with partner[s] == s keep their weights; the number of pairs varies between draws from 1 to 8. `old_place`: a permutation of the experts. `route_ids`: each row names 8 different experts; among the 48 tokens of one index of expert, no expert is named by more than 48 tokens.
All inputs are finite; a program needn't handle non-finite values.
Results may differ from a plain program's by a relative error of at most 0.0058.
Values may be sent and summed in bfloat16 or wider, within the bound.
A program may use at most 128 MiB of HBM per device.

v0:
```python
import jax
import jax.numpy as jnp
from jax import lax
from jax.sharding import PartitionSpec as P


def contract_last(left, right):
    return lax.dot_general(
        left, right, (((1,), (1,)), ((), ())), preferred_element_type=jnp.float32
    )


def exchange(partner, weights):
    groups = lax.axis_size("expert")

    def pieces_of(weight):
        rows, columns = weight.shape[1:]
        if rows % (8 * groups) == 0:
            return weight.reshape(groups, rows // groups, columns)
        return weight.reshape(groups, -1)

    spread = [
        lax.all_to_all(pieces_of(w), "expert", split_axis=0, concat_axis=0, tiled=True)
        for w in weights
    ]
    ordered = [jnp.take(s, partner, axis=0, mode="clip") for s in spread]
    arrived = [
        lax.all_to_all(o, "expert", split_axis=0, concat_axis=0, tiled=True) for o in ordered
    ]
    return tuple(a.reshape(w.shape) for a, w in zip(arrived, weights))


def body(tokens, route_ids, route_weight, partner, old_place, gate_weight, up_weight, down_weight):
    groups = lax.axis_size("expert")
    halves = lax.axis_size("narrow")
    me = lax.axis_index("expert")
    rows, part = tokens.shape
    new_gate, new_up, new_down = exchange(partner, (gate_weight, up_weight, down_weight))

    matches = route_ids[:, :, None] == old_place[None, None, :]
    share = jnp.sum(jnp.where(matches, route_weight[:, :, None].astype(jnp.float32), 0.0), axis=1)
    share = jnp.pad(share.astype(jnp.bfloat16), ((0, 0), (0, -groups % 128)))
    packed = jnp.concatenate([tokens, share], axis=1)
    full = lax.all_gather(packed, ("expert", "narrow")).reshape(groups, halves, rows, -1)
    everything = jnp.swapaxes(full[..., :part], 1, 2).reshape(groups * rows, halves * part)
    shares = lax.dynamic_slice_in_dim(full[:, 0, :, part:], me, 1, axis=2).reshape(groups * rows, 1)

    gate_sum = contract_last(everything, gate_weight[0])
    up_sum = contract_last(everything, up_weight[0])
    hidden = (jax.nn.silu(gate_sum) * up_sum).astype(jnp.bfloat16)
    hidden = lax.all_gather(hidden, "narrow", axis=1, tiled=True)
    produced = jnp.dot(hidden, down_weight[0], preferred_element_type=jnp.float32)
    weighted = produced.astype(jnp.bfloat16).astype(jnp.float32) * shares.astype(jnp.float32)
    layer_out = lax.psum_scatter(
        weighted.astype(jnp.bfloat16), "expert", scatter_dimension=0, tiled=True
    )
    return (layer_out, new_gate, new_up, new_down)


def solution(mesh):
    return jax.shard_map(
        body,
        mesh=mesh,
        in_specs=(
            P("expert", "narrow"),
            P("expert", None),
            P("expert", None),
            P(),
            P(),
            P("expert", "narrow", None),
            P("expert", "narrow", None),
            P("expert", None, "narrow"),
        ),
        out_specs=(
            P("expert", "narrow"),
            P("expert", "narrow", None),
            P("expert", "narrow", None),
            P("expert", None, "narrow"),
        ),
        check_vma=False,
    )
```

profile of v0, /device:TPU:15, one launch (start us, length us, event | category | flops | bytes accessed | tf_op | source)
XLA Modules:
  0.0 519.1 jit_solution(16433754501900889719)
XLA Ops:
  7.2 76.7 %all_to_all.30 = bf16[16,24,4096]{2,1,0:T(8,128)(2,1)} all-to-all(bf16[16,24,4096]{2,1,0:T(8,128)(2,1)} %bitcast.39), channel_id=1, replica_groups=mesh['expert'=16,'narrow'=2] {'expert'}, dimensions={0} | all-to-all | bytes 6291456 | tf_op jit(solution)/shard_map/all_to_all | solution.py:23
  83.9 74.9 %all_to_all.31 = bf16[16,24,4096]{2,1,0:T(8,128)(2,1)} all-to-all(bf16[16,24,4096]{2,1,0:T(8,128)(2,1)S(1)} %bitcast.40), channel_id=1, replica_groups=mesh['expert'=16,'narrow'=2] {'expert'}, dimensions={0} | all-to-all | bytes 6291456 | tf_op jit(solution)/shard_map/all_to_all | solution.py:23
  158.8 5.3 %all-to-all-start.4 = ((bf16[16,48,2048]{2,1,0:T(8,128)(2,1)}), bf16[16,48,2048]{2,1,0:T(8,128)(2,1)S(1)}, u32[]{:S(2)}, u32[]{:S(2)}) async-start(bf16[16,48,2048]{2,1,0:T(8,128)(2,1)} %bitcast.41), calls=%async_computation.5 | async-start | bytes 6291456 | tf_op jit(solution)/shard_map/all_to_all | solution.py:23
  165.1 4.3 gather_fusion
  169.4 81.0 %all-to-all-done.4 = bf16[16,48,2048]{2,1,0:T(8,128)(2,1)S(1)} async-done(((bf16[16,48,2048]{2,1,0:T(8,128)(2,1)}), bf16[16,48,2048]{2,1,0:T(8,128)(2,1)S(1)}, u32[]{:S(2)}, u32[]{:S(2)}) %all-to-all-start.4) | async-done | bytes 3145760 | tf_op jit(solution)/shard_map/all_to_all | solution.py:23
  250.5 1.7 copy-done
  252.1 5.2 %all-to-all-start.1 = ((bf16[16,24,4096]{2,1,0:T(8,128)(2,1)}), bf16[16,24,4096]{2,1,0:T(8,128)(2,1)S(1)}, u32[]{:S(2)}, u32[]{:S(2)}) async-start(bf16[16,24,4096]{2,1,0:T(8,128)(2,1)} %gather_fusion), calls=%async_computation.2 | async-start | bytes 6291456 | tf_op jit(solution)/shard_map/all_to_all | solution.py:28
  257.3 4.3 gather_fusion.1
  261.6 72.3 %all-to-all-done.1 = bf16[16,24,4096]{2,1,0:T(8,128)(2,1)S(1)} async-done(((bf16[16,24,4096]{2,1,0:T(8,128)(2,1)}), bf16[16,24,4096]{2,1,0:T(8,128)(2,1)S(1)}, u32[]{:S(2)}, u32[]{:S(2)}) %all-to-all-start.1) | async-done | bytes 3145760 | tf_op jit(solution)/shard_map/all_to_all | solution.py:28
  333.9 4.7 all-to-all-start.3
  338.7 3.4 slice.14
  342.1 13.5 %copy.21 = bf16[16,2,48,2048]{3,1,2,0:T(2,128)(2,1)S(1)} copy(bf16[16,2,48,2048]{3,2,1,0:T(8,128)(2,1)S(1)} %slice.14) | data formatting | bytes 12582912
  355.6 4.1 copy.25
  359.7 3.4 fusion.3
  363.1 4.3 fusion.10
  367.4 4.3 gather_fusion.2
  371.7 36.9 %all-to-all-done.3 = bf16[16,24,4096]{2,1,0:T(8,128)(2,1)} async-done(((bf16[16,24,4096]{2,1,0:T(8,128)(2,1)}), bf16[16,24,4096]{2,1,0:T(8,128)(2,1)}, u32[]{:S(2)}, u32[]{:S(2)}) %all-to-all-start.3) | async-done | bytes 3145760 | tf_op jit(solution)/shard_map/all_to_all | solution.py:28
  408.6 4.9 all-to-all-start.5
  415.1 6.5 %multiply_convert_fusion = bf16[768,2048]{1,0:T(8,128)(2,1)} fusion(f32[768]{0:T(1024)S(1)} %reshape.56, bf16[768,768]{1,0:T(8,128)(2,1)} %all-gather.4.cloned.1.call-done, bf16[1,768,2048]{2,1,0:T(8,128)(2,1)} %param.15), kind=kOutput, calls=%fused_computation.3 | convolution fusion | flops 2422210560 | bytes 7474176 | tf_op jit(solution)/shard_map/dot_general | solution.py:52
  421.7 79.2 %all-to-all-done.5 = bf16[16,48,2048]{2,1,0:T(8,128)(2,1)} async-done(((bf16[16,48,2048]{2,1,0:T(8,128)(2,1)}), bf16[16,48,2048]{2,1,0:T(8,128)(2,1)}, u32[]{:S(2)}, u32[]{:S(2)}) %all-to-all-start.5) | async-done | bytes 3145760 | tf_op jit(solution)/shard_map/all_to_all | solution.py:28
  500.9 2.1 reduce-scatter.2.cloned.1.call-done
  503.1 1.7 copy.29
  504.7 3.9 copy.30
  508.6 4.0 copy.31
  (34 shorter events, 2.6 us)
Async XLA Ops:
  7.2 76.7 %copy-start.2 = (bf16[1,384,4096]{2,1,0:T(8,128)(2,1)S(1)}, bf16[1,384,4096]{2,1,0:T(8,128)(2,1)}, u32[]{:S(2)}) copy-start(bf16[1,384,4096]{2,1,0:T(8,128)(2,1)} %param.14) | copy-start | bytes 9437188
  158.8 5.4 %copy-start.6 = (bf16[48,8]{0,1:T(8,128)(2,1)S(1)}, bf16[48,8]{0,1:T(8,128)(2,1)}, u32[]{:S(2)}) copy-start(bf16[48,8]{0,1:T(8,128)(2,1)} %param.10) | copy-start | bytes 2308
  158.8 5.4 %copy-start.5 = (s32[48,8]{0,1:T(8,128)S(1)}, s32[48,8]{0,1:T(8,128)}, u32[]{:S(2)}) copy-start(s32[48,8]{0,1:T(8,128)} %param.9) | copy-start | bytes 4612
  158.8 5.4 %copy-start.7 = (s32[16]{0:T(128)S(1)}, s32[16]{0:T(128)}, u32[]{:S(2)}) copy-start(s32[16]{0:T(128)} %param.12) | copy-start | bytes 196
  158.8 5.6 %copy-start.4 = (bf16[48,2048]{1,0:T(8,128)(2,1)S(1)}, bf16[48,2048]{1,0:T(8,128)(2,1)}, u32[]{:S(2)}) copy-start(bf16[48,2048]{1,0:T(8,128)(2,1)} %param.8) | copy-start | bytes 589828
  158.8 6.4 %copy-start.8 = (s32[16]{0:T(128)S(1)}, s32[16]{0:T(128)}, u32[]{:S(2)}) copy-start(s32[16]{0:T(128)} %param.11) | copy-start | bytes 196
  158.8 91.7 %all-to-all-start.4 = ((bf16[16,48,2048]{2,1,0:T(8,128)(2,1)}), bf16[16,48,2048]{2,1,0:T(8,128)(2,1)S(1)}, u32[]{:S(2)}, u32[]{:S(2)}) async-start(bf16[16,48,2048]{2,1,0:T(8,128)(2,1)} %bitcast.41), calls=%async_computation.5 | async-start | bytes 6291456 | tf_op jit(solution)/shard_map/all_to_all | solution.py:23
  164.1 174.6 %all-gather.6.cloned.1.call-start = ((), (), s32[]{:S(2)}) async-start(), calls=%async_computation.9 | async-start | bytes 6893568 | tf_op jit(solution)/shard_map/all_gather | solution.py:44
  250.4 1.7 copy-start
  252.1 81.8 %all-to-all-start.1 = ((bf16[16,24,4096]{2,1,0:T(8,128)(2,1)}), bf16[16,24,4096]{2,1,0:T(8,128)(2,1)S(1)}, u32[]{:S(2)}, u32[]{:S(2)}) async-start(bf16[16,24,4096]{2,1,0:T(8,128)(2,1)} %gather_fusion), calls=%async_computation.2 | async-start | bytes 6291456 | tf_op jit(solution)/shard_map/all_to_all | solution.py:28
  333.9 74.7 %all-to-all-start.3 = ((bf16[16,24,4096]{2,1,0:T(8,128)(2,1)}), bf16[16,24,4096]{2,1,0:T(8,128)(2,1)}, u32[]{:S(2)}, u32[]{:S(2)}) async-start(bf16[16,24,4096]{2,1,0:T(8,128)(2,1)} %gather_fusion.1), calls=%async_computation.4 | async-start | bytes 6291456 | tf_op jit(solution)/shard_map/all_to_all | solution.py:28
  338.6 76.5 %all-gather.4.cloned.1.call-start = ((), (), s32[]{:S(2)}) async-start(), calls=%async_computation.7 | async-start | bytes 1769472 | tf_op jit(solution)/shard_map/all_gather | solution.py:51
  355.6 4.1 copy-start.1
  359.7 3.4 copy-start.3
  408.6 92.3 %all-to-all-start.5 = ((bf16[16,48,2048]{2,1,0:T(8,128)(2,1)}), bf16[16,48,2048]{2,1,0:T(8,128)(2,1)}, u32[]{:S(2)}, u32[]{:S(2)}) async-start(bf16[16,48,2048]{2,1,0:T(8,128)(2,1)} %gather_fusion.2), calls=%async_computation.6 | async-start | bytes 6291456 | tf_op jit(solution)/shard_map/all_to_all | solution.py:28
  413.5 89.5 %reduce-scatter.2.cloned.1.call-start = ((), (), s32[]{:S(2)}) async-start(), calls=%async_computation.8 | async-start | bytes 3342336 | tf_op jit(solution)/shard_map/reduce_scatter | solution.py:54
Sparse Core Ops, SparseCore 0:
  167.9 117.9 all-gather.5
  367.6 22.4 all-gather.3
  421.8 81.2 reduce-scatter.1
where the time goes:
time: 524 us; the launch traced here: 519 us
  waiting for transfers between devices  272 us (52%)
  blocking collectives  152 us (29%)
  local copies, waits for them, and re-layouts  46.5 us (9%)
  starting transfers between devices  20.4 us (4%)
  matrix products  14.3 us (3%)
  between operations  13.9 us (3%)
    all_to_all x3, waiting for transfers between devices, exchange(): lax.all_to_all(o, 'expert', split_axis=0, concat_axis=0, tiled=True)  188 us
    all_to_all x2, blocking collectives, exchange(): lax.all_to_all(pieces_of(w), 'expert', split_axis=0, concat_axis=0, tiled...  152 us
    all_to_all x1, waiting for transfers between devices, exchange(): lax.all_to_all(pieces_of(w), 'expert', split_axis=0, concat_axis=0, tiled...  81 us
    unnamed x25, local copies, waits for them, and re-layouts  29.1 us
    all_to_all x3, starting transfers between devices, exchange(): lax.all_to_all(o, 'expert', split_axis=0, concat_axis=0, tiled=True)  14.8 us
    gather x3, local copies, waits for them, and re-layouts, exchange(): ordered = [jnp.take(s, partner, axis=0, mode='clip') for s in spread]  12.9 us
  transfers between devices with their start and end apart: 7, of which 5 were waited for; matrix products, arithmetic and copies ran while one was open for 10% of the time, Pallas kernels for 0%

commit v1 on v0

--- a/solution.py
+++ b/solution.py
@@ -10,7 +10,7 @@
     )
 
 
-def exchange(partner, weights):
+def spread_out(partner, weights):
     groups = lax.axis_size("expert")
 
     def pieces_of(weight):
@@ -23,11 +23,12 @@
         lax.all_to_all(pieces_of(w), "expert", split_axis=0, concat_axis=0, tiled=True)
         for w in weights
     ]
-    ordered = [jnp.take(s, partner, axis=0, mode="clip") for s in spread]
-    arrived = [
-        lax.all_to_all(o, "expert", split_axis=0, concat_axis=0, tiled=True) for o in ordered
-    ]
-    return tuple(a.reshape(w.shape) for a, w in zip(arrived, weights))
+    return [jnp.take(s, partner, axis=0, mode="clip") for s in spread]
+
+
+def collect(ordered, weight):
+    arrived = lax.all_to_all(ordered, "expert", split_axis=0, concat_axis=0, tiled=True)
+    return arrived.reshape(weight.shape)
 
 
 def body(tokens, route_ids, route_weight, partner, old_place, gate_weight, up_weight, down_weight):
@@ -35,7 +36,7 @@
     halves = lax.axis_size("narrow")
     me = lax.axis_index("expert")
     rows, part = tokens.shape
-    new_gate, new_up, new_down = exchange(partner, (gate_weight, up_weight, down_weight))
+    gate_order, up_order, down_order = spread_out(partner, (gate_weight, up_weight, down_weight))
 
     matches = route_ids[:, :, None] == old_place[None, None, :]
     share = jnp.sum(jnp.where(matches, route_weight[:, :, None].astype(jnp.float32), 0.0), axis=1)
@@ -48,12 +49,17 @@
     gate_sum = contract_last(everything, gate_weight[0])
     up_sum = contract_last(everything, up_weight[0])
     hidden = (jax.nn.silu(gate_sum) * up_sum).astype(jnp.bfloat16)
+    hidden, gate_order = lax.optimization_barrier((hidden, gate_order))
+    new_gate = collect(gate_order, gate_weight)
     hidden = lax.all_gather(hidden, "narrow", axis=1, tiled=True)
     produced = jnp.dot(hidden, down_weight[0], preferred_element_type=jnp.float32)
     weighted = produced.astype(jnp.bfloat16).astype(jnp.float32) * shares.astype(jnp.float32)
-    layer_out = lax.psum_scatter(
-        weighted.astype(jnp.bfloat16), "expert", scatter_dimension=0, tiled=True
+    weighted, up_order, down_order = lax.optimization_barrier(
+        (weighted.astype(jnp.bfloat16), up_order, down_order)
     )
+    layer_out = lax.psum_scatter(weighted, "expert", scatter_dimension=0, tiled=True)
+    new_up = collect(up_order, up_weight)
+    new_down = collect(down_order, down_weight)
     return (layer_out, new_gate, new_up, new_down)
 
 

time: 524 us -> 524 us (level)
  waiting for transfers between devices: 272 us -> 262 us
  blocking collectives: 152 us -> 160 us
    all_to_all x4, waiting for transfers between devices: 269 us -> 245 us  [the longest x2 125 us: collect(): lax.all_to_all(ordered, 'expert', split_axis=0, concat_axis=0, tiled=True)]
    all_gather x1, waiting for transfers between devices: 0.01 us -> 14.1 us  [body(): hidden = lax.all_gather(hidden, 'narrow', axis=1, tiled=True)]
    all_to_all x2, blocking collectives: 152 us -> 160 us  [the longest x1 85.2 us: spread_out(): lax.all_to_all(pieces_of(w), 'expert', split_axis=0, concat_axis=0, tiled...]
    unnamed x25 -> x27, local copies, waits for them, and re-layouts: 29.1 us -> 28.2 us
  transfers between devices with their start and end apart: 7 -> 7, of which waited for: 5 -> 6; matrix products, arithmetic and copies ran while one was open for 10% -> 10% of each run, Pallas kernels for 0% -> 0%
where the time goes in v1:
time: 524 us; the launch traced here: 519 us
  waiting for transfers between devices  262 us (50%)
  blocking collectives  160 us (31%)
  local copies, waits for them, and re-layouts  45.7 us (9%)
  starting transfers between devices  22.3 us (4%)
  matrix products  14.2 us (3%)
  between operations  13.9 us (3%)
    all_to_all x2, waiting for transfers between devices, collect(): lax.all_to_all(ordered, 'expert', split_axis=0, concat_axis=0, tiled=True)  125 us
    all_to_all x2, waiting for transfers between devices, spread_out(): lax.all_to_all(pieces_of(w), 'expert', split_axis=0, concat_axis=0, tiled...  120 us
    all_to_all x1, blocking collectives, spread_out(): lax.all_to_all(pieces_of(w), 'expert', split_axis=0, concat_axis=0, tiled...  85.2 us
    all_to_all x1, blocking collectives, collect(): lax.all_to_all(ordered, 'expert', split_axis=0, concat_axis=0, tiled=True)  74.8 us
    unnamed x27, local copies, waits for them, and re-layouts  28.2 us
    all_gather x1, waiting for transfers between devices, body(): hidden = lax.all_gather(hidden, 'narrow', axis=1, tiled=True)  14.1 us
    gather x3, local copies, waits for them, and re-layouts, spread_out(): return [jnp.take(s, partner, axis=0, mode='clip') for s in spread]  12.9 us
    all_to_all x2, starting transfers between devices, spread_out(): lax.all_to_all(pieces_of(w), 'expert', split_axis=0, concat_axis=0, tiled...  11.9 us
  transfers between devices with their start and end apart: 7, of which 6 were waited for; matrix products, arithmetic and copies ran while one was open for 10% of the time, Pallas kernels for 0%

profile of v1, /device:TPU:15, one launch (start us, length us, event | category | flops | bytes accessed | tf_op | source)
XLA Modules:
  0.0 519.4 jit_solution(17015563180866183330)
XLA Ops:
  7.2 6.7 %all-to-all-start = ((bf16[16,24,4096]{2,1,0:T(8,128)(2,1)}), bf16[16,24,4096]{2,1,0:T(8,128)(2,1)S(1)}, u32[]{:S(2)}, u32[]{:S(2)}) async-start(bf16[16,24,4096]{2,1,0:T(8,128)(2,1)} %bitcast.40), calls=%async_computation | async-start | bytes 6291456 | tf_op jit(solution)/shard_map/all_to_all | solution.py:23
  14.9 82.9 %all-to-all-done = bf16[16,24,4096]{2,1,0:T(8,128)(2,1)S(1)} async-done(((bf16[16,24,4096]{2,1,0:T(8,128)(2,1)}), bf16[16,24,4096]{2,1,0:T(8,128)(2,1)S(1)}, u32[]{:S(2)}, u32[]{:S(2)}) %all-to-all-start) | async-done | bytes 3145760 | tf_op jit(solution)/shard_map/all_to_all | solution.py:23
  97.8 85.2 %all_to_all.30 = bf16[16,24,4096]{2,1,0:T(8,128)(2,1)} all-to-all(bf16[16,24,4096]{2,1,0:T(8,128)(2,1)} %bitcast.41), channel_id=1, replica_groups=mesh['expert'=16,'narrow'=2] {'expert'}, dimensions={0} | all-to-all | bytes 6291456 | tf_op jit(solution)/shard_map/all_to_all | solution.py:23
  182.9 5.2 %all-to-all-start.2 = ((bf16[16,48,2048]{2,1,0:T(8,128)(2,1)}), bf16[16,48,2048]{2,1,0:T(8,128)(2,1)S(1)}, u32[]{:S(2)}, u32[]{:S(2)}) async-start(bf16[16,48,2048]{2,1,0:T(8,128)(2,1)} %bitcast.42), calls=%async_computation.2 | async-start | bytes 6291456 | tf_op jit(solution)/shard_map/all_to_all | solution.py:23
  188.2 4.3 gather_fusion
  192.5 3.4 slice.14
  195.9 13.5 %copy.21 = bf16[16,2,48,2048]{3,1,2,0:T(2,128)(2,1)S(1)} copy(bf16[16,2,48,2048]{3,2,1,0:T(8,128)(2,1)S(1)} %slice.14) | data formatting | bytes 12582912
  209.4 4.1 copy.25
  213.5 3.4 fusion.3
  216.9 4.3 fusion.10
  221.2 36.8 %all-to-all-done.2 = bf16[16,48,2048]{2,1,0:T(8,128)(2,1)S(1)} async-done(((bf16[16,48,2048]{2,1,0:T(8,128)(2,1)}), bf16[16,48,2048]{2,1,0:T(8,128)(2,1)S(1)}, u32[]{:S(2)}, u32[]{:S(2)}) %all-to-all-start.2) | async-done | bytes 3145760 | tf_op jit(solution)/shard_map/all_to_all | solution.py:23
  259.7 4.9 all-to-all-start.3
  265.4 4.3 gather_fusion.1
  269.7 4.3 gather_fusion.2
  275.4 14.1 %all-gather.4.cloned.1.call-done = bf16[768,768]{1,0:T(8,128)(2,1)} async-done(((bf16[768,384]{1,0:T(8,128)(2,1)}), bf16[768,768]{1,0:T(8,128)(2,1)}) %all-gather.4.cloned.1.call-update) | async-done | bytes 1179664 | tf_op jit(solution)/shard_map/all_gather | solution.py:54
  289.5 6.5 %multiply_convert_fusion = bf16[768,2048]{1,0:T(8,128)(2,1)} fusion(f32[768]{0:T(1024)S(1)} %reshape.56, bf16[768,768]{1,0:T(8,128)(2,1)} %all-gather.4.cloned.1.call-done, bf16[1,768,2048]{2,1,0:T(8,128)(2,1)} %param.15), kind=kOutput, calls=%fused_computation.3 | convolution fusion | flops 2422210560 | bytes 7474176 | tf_op jit(solution)/shard_map/dot_general | solution.py:55
  296.0 38.5 %all-to-all-done.3 = bf16[16,24,4096]{2,1,0:T(8,128)(2,1)S(1)} async-done(((bf16[16,24,4096]{2,1,0:T(8,128)(2,1)}), bf16[16,24,4096]{2,1,0:T(8,128)(2,1)S(1)}, u32[]{:S(2)}, u32[]{:S(2)}) %all-to-all-start.3) | async-done | bytes 3145760 | tf_op jit(solution)/shard_map/all_to_all | solution.py:30
  334.5 74.8 %all_to_all.31 = bf16[16,24,4096]{2,1,0:T(8,128)(2,1)} all-to-all(bf16[16,24,4096]{2,1,0:T(8,128)(2,1)} %gather_fusion.1), channel_id=1, replica_groups=mesh['expert'=16,'narrow'=2] {'expert'}, dimensions={0} | all-to-all | bytes 6291456 | tf_op jit(solution)/shard_map/all_to_all | solution.py:30
  409.3 5.2 %all-to-all-start.5 = ((bf16[16,48,2048]{2,1,0:T(8,128)(2,1)}), bf16[16,48,2048]{2,1,0:T(8,128)(2,1)}, u32[]{:S(2)}, u32[]{:S(2)}) async-start(bf16[16,48,2048]{2,1,0:T(8,128)(2,1)} %gather_fusion.2), calls=%async_computation.6 | async-start | bytes 6291456 | tf_op jit(solution)/shard_map/all_to_all | solution.py:30
  415.2 86.9 %all-to-all-done.5 = bf16[16,48,2048]{2,1,0:T(8,128)(2,1)} async-done(((bf16[16,48,2048]{2,1,0:T(8,128)(2,1)}), bf16[16,48,2048]{2,1,0:T(8,128)(2,1)}, u32[]{:S(2)}, u32[]{:S(2)}) %all-to-all-start.5) | async-done | bytes 3145760 | tf_op jit(solution)/shard_map/all_to_all | solution.py:30
  502.1 2.0 reduce-scatter.2.cloned.1.call-done
  504.2 1.7 copy.29
  507.2 1.7 copy.30
  508.9 4.0 copy.31
  (36 shorter events, 6.8 us)
Async XLA Ops:
  7.2 6.8 %copy-start.7 = (bf16[48,8]{0,1:T(8,128)(2,1)S(1)}, bf16[48,8]{0,1:T(8,128)(2,1)}, u32[]{:S(2)}) copy-start(bf16[48,8]{0,1:T(8,128)(2,1)} %param.10) | copy-start | bytes 2308
  7.2 6.8 %copy-start.6 = (s32[48,8]{0,1:T(8,128)S(1)}, s32[48,8]{0,1:T(8,128)}, u32[]{:S(2)}) copy-start(s32[48,8]{0,1:T(8,128)} %param.9) | copy-start | bytes 4612
  7.2 6.8 %copy-start.8 = (s32[16]{0:T(128)S(1)}, s32[16]{0:T(128)}, u32[]{:S(2)}) copy-start(s32[16]{0:T(128)} %param.12) | copy-start | bytes 196
  7.2 7.0 %copy-start.5 = (bf16[48,2048]{1,0:T(8,128)(2,1)S(1)}, bf16[48,2048]{1,0:T(8,128)(2,1)}, u32[]{:S(2)}) copy-start(bf16[48,2048]{1,0:T(8,128)(2,1)} %param.8) | copy-start | bytes 589828
  7.2 90.6 %all-to-all-start = ((bf16[16,24,4096]{2,1,0:T(8,128)(2,1)}), bf16[16,24,4096]{2,1,0:T(8,128)(2,1)S(1)}, u32[]{:S(2)}, u32[]{:S(2)}) async-start(bf16[16,24,4096]{2,1,0:T(8,128)(2,1)} %bitcast.40), calls=%async_computation | async-start | bytes 6291456 | tf_op jit(solution)/shard_map/all_to_all | solution.py:23
  13.9 178.6 %all-gather.6.cloned.1.call-start = ((), (), s32[]{:S(2)}) async-start(), calls=%async_computation.9 | async-start | bytes 6893568 | tf_op jit(solution)/shard_map/all_gather | solution.py:45
  97.8 85.2 %copy-start.1 = (bf16[16,24,4096]{2,1,0:T(8,128)(2,1)}, bf16[16,24,4096]{2,1,0:T(8,128)(2,1)S(1)}, u32[]{:S(2)}) copy-start(bf16[16,24,4096]{2,1,0:T(8,128)(2,1)S(1)} %all-to-all-done) | copy-start | bytes 9437188
  182.9 5.2 %copy-start.9 = (s32[16]{0:T(128)S(1)}, s32[16]{0:T(128)}, u32[]{:S(2)}) copy-start(s32[16]{0:T(128)} %param.11) | copy-start | bytes 196
  182.9 75.1 %all-to-all-start.2 = ((bf16[16,48,2048]{2,1,0:T(8,128)(2,1)}), bf16[16,48,2048]{2,1,0:T(8,128)(2,1)S(1)}, u32[]{:S(2)}, u32[]{:S(2)}) async-start(bf16[16,48,2048]{2,1,0:T(8,128)(2,1)} %bitcast.42), calls=%async_computation.2 | async-start | bytes 6291456 | tf_op jit(solution)/shard_map/all_to_all | solution.py:23
  209.4 4.1 copy-start.3
  213.5 3.4 copy-start.4
  258.1 1.7 copy-start
  259.7 74.8 %all-to-all-start.3 = ((bf16[16,24,4096]{2,1,0:T(8,128)(2,1)}), bf16[16,24,4096]{2,1,0:T(8,128)(2,1)S(1)}, u32[]{:S(2)}, u32[]{:S(2)}) async-start(bf16[16,24,4096]{2,1,0:T(8,128)(2,1)} %gather_fusion), calls=%async_computation.4 | async-start | bytes 6291456 | tf_op jit(solution)/shard_map/all_to_all | solution.py:30
  264.6 24.8 %all-gather.4.cloned.1.call-start = ((), (), s32[]{:S(2)}) async-start(), calls=%async_computation.7 | async-start | bytes 1769472 | tf_op jit(solution)/shard_map/all_gather | solution.py:54
  409.3 92.8 %all-to-all-start.5 = ((bf16[16,48,2048]{2,1,0:T(8,128)(2,1)}), bf16[16,48,2048]{2,1,0:T(8,128)(2,1)}, u32[]{:S(2)}, u32[]{:S(2)}) async-start(bf16[16,48,2048]{2,1,0:T(8,128)(2,1)} %gather_fusion.2), calls=%async_computation.6 | async-start | bytes 6291456 | tf_op jit(solution)/shard_map/all_to_all | solution.py:30
  414.5 89.7 %reduce-scatter.2.cloned.1.call-start = ((), (), s32[]{:S(2)}) async-start(), calls=%async_computation.8 | async-start | bytes 3342336 | tf_op jit(solution)/shard_map/reduce_scatter | solution.py:60
  504.2 3.0 copy-start.2
Sparse Core Ops, SparseCore 0:
  18.2 113.9 all-gather.5
  267.0 22.4 all-gather.3
  419.7 84.4 reduce-scatter.1
